TPU v7x, 32 devices: a whole 2x2x4 slice. The times are simulated.
32 devices in a mesh: replica: 2 (over y), ep: 8 (over z, x), tp: 2 (over core).
Axes of the slice: x: 2, y: 2, z: 4, core: 2. Of those that a mesh axis runs over, the one named last changes fastest.
Arguments:
- residual_in: bfloat16 [1024, 3584], P(('replica', 'ep')), parts along dimension 0, may hold values from -6 to 6
- dense_terms: bfloat16 [2, 1024, 3584], P('tp', ('replica', 'ep')), parts along dimension 1, may hold values from -6 to 6
- norm_gain: float32 [3584], replicated, may hold values from 0.1 to 1.9
- router_weight: bfloat16 [3584, 64], P('tp'), may hold values from -0.09375 to 0.09375
- routes: int32 [1024, 8], P(('replica', 'ep')), parts along dimension 0, may hold values from 0 to 63, all different within a row; in each aligned block of 64 rows (0 to 63, 64 to 127, ...) at most 12 rows name the same one
- placement: int32 [64], replicated, may hold values from 0 to 63, each once
- up_weight: bfloat16 [3584, 65536], P('tp', 'ep'), may hold values from -0.09375 to 0.09375
- down_weight: bfloat16 [65536, 3584], P('ep', 'tp'), may hold values from -0.1875 to 0.1875
Outputs:
- mixed: bfloat16 [1024, 3584], P(('replica', 'ep'), 'tp'), parts along dimension 0
There are 2 independent parts, one for each index of `replica`. A program takes and returns all parts, laid end to end along the dimension named above; an argument that names none is the same for every part. Nothing has to cross between parts.
Inputs may be any that keep to these rules, and one draw needn't show every extreme that they name: `routes`: in the rows of one index of ep no expert is named by more than 12 rows. `placement`: each slot holds exactly one expert.
All inputs are finite; a program needn't handle non-finite values.
Results may differ from a plain program's by a relative error of at most 0.011.
Values may be sent and summed in bfloat16 or wider, within the bound.
A program may use at most 256 MiB of HBM per device.

v0:
```python
import jax
import jax.numpy as jnp
from jax import lax
from jax.sharding import PartitionSpec as P

FF_E = 1024
CAP = 12


def on_device(
    residual_in, dense_terms, norm_gain, router_weight, routes, placement, up_weight, down_weight
):
    half_width = up_weight.shape[0]
    columns = up_weight.shape[1]
    tok_rows = residual_in.shape[0]
    experts = placement.shape[0]
    peers = lax.axis_size("ep")
    start = lax.axis_index("tp") * half_width
    local_slots = max(1, columns // FF_E)
    span = min(FF_E, columns)
    capacity = min(tok_rows, CAP * local_slots)
    res_full = residual_in.astype(jnp.float32)
    router_f = router_weight.astype(jnp.float32)
    dense_mine = dense_terms[0].astype(jnp.float32)
    dense_full = lax.psum(dense_mine.astype(jnp.bfloat16), "tp").astype(jnp.float32)
    state = res_full + dense_full
    mean_sq = jnp.mean(state * state, axis=-1, keepdims=True)
    normed = state * lax.rsqrt(mean_sq + 1e-06) * norm_gain
    normed_half = lax.dynamic_slice_in_dim(normed, start, half_width, 1)
    state_half = lax.dynamic_slice_in_dim(state, start, half_width, 1)
    part_logits = jnp.dot(normed_half, router_f, precision=lax.Precision.HIGHEST)
    logits = lax.psum(part_logits, "tp")
    scores = jax.nn.sigmoid(logits)
    expert_ids = jnp.arange(experts, dtype=jnp.int32)
    onehot = routes[:, :, None] == expert_ids[None, None, :]
    chosen = jnp.sum(jnp.where(onehot, scores[:, None, :], 0.0), axis=-1)
    route_weight = 2.827 * chosen / jnp.sum(chosen, axis=-1, keepdims=True)
    expert_gate = jnp.sum(jnp.where(onehot, route_weight[:, :, None], 0.0), axis=1)
    slot_table = (placement[:, None] == expert_ids[None, :]).astype(jnp.float32)
    slot_gate = jnp.dot(expert_gate, slot_table, precision=lax.Precision.HIGHEST)
    peer_ids = jnp.arange(peers, dtype=jnp.int32)
    slot_of_peer = (
        peer_ids[:, None] * columns // FF_E + jnp.arange(local_slots, dtype=jnp.int32)[None, :]
    )
    pick_table = (slot_of_peer[:, :, None] == expert_ids[None, None, :]).astype(jnp.float32)
    peer_gates = jnp.einsum("ts,pls->tpl", slot_gate, pick_table, precision=lax.Precision.HIGHEST)
    need = (jnp.sum(peer_gates, axis=-1) > 0.0).astype(jnp.int32)
    position = jnp.cumsum(need, axis=0) - 1
    slot_pos = jnp.arange(capacity, dtype=jnp.int32)
    selector = (need.T[:, None, :] == 1) & (position.T[:, None, :] == slot_pos[None, :, None])
    select_b = selector.astype(jnp.bfloat16)
    select_f = selector.astype(jnp.float32)
    send_gates = jnp.einsum("pct,tpl->pcl", select_f, peer_gates, precision=lax.Precision.HIGHEST)
    rows_bf = normed_half.astype(jnp.bfloat16)
    send_rows = jnp.einsum(
        "pct,tf->pcf", select_b, rows_bf, preferred_element_type=jnp.float32
    ).astype(jnp.bfloat16)
    rows_in = lax.all_to_all(send_rows, "ep", split_axis=0, concat_axis=0, tiled=True)
    gates_in = lax.all_to_all(
        send_gates.astype(jnp.bfloat16), "ep", split_axis=0, concat_axis=0, tiled=True
    ).astype(send_gates.dtype)
    part_pre = jnp.einsum("sif,fh->sih", rows_in, up_weight, preferred_element_type=jnp.float32)
    pre = lax.psum(part_pre.astype(jnp.bfloat16), "tp").astype(jnp.float32)
    column_gate = jnp.repeat(gates_in, span, axis=2)
    gated = (jax.nn.silu(pre) * column_gate).astype(jnp.bfloat16)
    result = jnp.einsum(
        "sih,hf->sif", gated, down_weight, preferred_element_type=jnp.float32
    ).astype(jnp.bfloat16)
    returned = lax.all_to_all(result, "ep", split_axis=0, concat_axis=0, tiled=True)
    expert_sum = jnp.einsum("pct,pcf->tf", select_b, returned, preferred_element_type=jnp.float32)
    return (state_half + expert_sum).astype(jnp.bfloat16)


def solution(mesh):
    in_specs = (
        P(("replica", "ep"), None),
        P("tp", ("replica", "ep"), None),
        P(),
        P("tp", None),
        P(("replica", "ep"), None),
        P(),
        P("tp", "ep"),
        P("ep", "tp"),
    )
    out_specs = P(("replica", "ep"), "tp")
    return jax.shard_map(
        on_device, mesh=mesh, in_specs=in_specs, out_specs=out_specs, check_vma=False
    )
```

profile of v0, /device:TPU:0, one launch (start us, length us, event | category | flops | bytes accessed | tf_op | source)
XLA Modules:
  0.0 235.7 jit_solution(13714593080130373548)
XLA Ops:
  6.5 0.0 copy-start
  6.5 0.0 all-reduce.3.cloned.1.call-start
  6.5 0.7 all-reduce.3.cloned.1.call-update
  7.3 0.0 all-reduce.5.cloned.1.call-start
  7.3 0.8 copy.19
  8.1 0.8 dynamic-slice
  8.9 0.1 iota_add_fusion
  8.9 22.1 %all-reduce.3.cloned.1.call-done = bf16[64,3584]{1,0:T(8,128)(2,1)} async-done(((bf16[64,3584]{1,0:T(8,128)(2,1)}), bf16[64,3584]{1,0:T(8,128)(2,1)}) %all-reduce.3.cloned.1.call-update) | async-done | bytes 458768 | tf_op jit(solution)/shard_map/psum | solution.py:25
  31.1 1.4 multiply_reduce_fusion
  32.5 0.0 copy-done
  32.5 0.4 fusion.21
  32.9 3.5 %psum.22 = f32[64,64]{1,0:T(8,128)S(1)} all-reduce(f32[64,64]{1,0:T(8,128)S(1)} %fusion.21), channel_id=1, replica_groups=mesh['replica'=2,'ep'=8,'tp'=2] {'tp'}, use_global_device_ids=true, to_apply=%region_2.0 | all-reduce | flops 4096 | bytes 32768 | tf_op jit(solution)/shard_map/psum | solution.py:32
  36.4 1.0 select_reduce_fusion
  37.4 0.1 multiply_divide_fusion
  37.5 0.2 select_reduce_fusion.2
  37.8 0.9 convolution_bitcast_fusion.1
  38.6 0.2 fusion.45
  38.9 0.1 copy.20
  39.0 0.1 reduce_window_sum.11
  39.1 0.1 copy.21
  39.1 0.9 convolution_convert_fusion
  40.0 48.6 %all_to_all.15 = bf16[8,64,1792]{2,1,0:T(8,128)(2,1)S(1)} all-to-all(bf16[8,64,1792]{2,1,0:T(8,128)(2,1)S(1)} %convolution_convert_fusion), channel_id=1, replica_groups=mesh['replica'=2,'ep'=8,'tp'=2] {'ep'}, dimensions={0} | all-to-all | bytes 3670016 | tf_op jit(solution)/shard_map/all_to_all | solution.py:58
  88.6 22.7 %fusion.9 = bf16[8,64,8192]{2,1,0:T(8,128)(2,1)} fusion(bf16[8,64,1792]{2,1,0:T(8,128)(2,1)S(1)} %all_to_all.15, bf16[1792,8192]{1,0:T(8,128)(2,1)} %param.14), kind=kOutput, calls=%fused_computation.11 | convolution fusion | flops 15036579840 | bytes 39583744 | tf_op jit(solution)/shard_map/sif,fh->sih/dot_general | solution.py:62
  111.3 0.0 all-reduce.5.cloned.1.call-update
  111.3 0.4 fusion.46
  111.7 0.1 reshape.101
  111.8 9.9 %all_to_all.16 = bf16[8,2,256]{2,1,0:T(2,128)(2,1)S(1)} all-to-all(bf16[8,2,256]{2,1,0:T(2,128)(2,1)S(1)} %reshape.101), channel_id=1, replica_groups=mesh['replica'=2,'ep'=8,'tp'=2] {'ep'}, dimensions={0} | all-to-all | bytes 16384 | tf_op jit(solution)/shard_map/all_to_all | solution.py:59
  121.7 0.1 reshape.102
  121.8 0.1 copy.24
  121.9 7.6 %broadcast_in_dim.27 = f32[8,64,8,1024]{3,2,1,0:T(8,128)} broadcast(f32[8,64,8]{2,1,0:T(8,128)S(1)} %copy.24), dimensions={0,1,2} | broadcast | bytes 16793600 | tf_op jit(solution)/shard_map/broadcast_in_dim | solution.py:64
  129.5 19.0 %reshape.95 = f32[8,64,8192]{2,1,0:T(8,128)} reshape(f32[8,64,8,1024]{3,2,1,0:T(8,128)} %broadcast_in_dim.27) | data formatting | bytes 33554432 | tf_op jit(solution)/shard_map/reshape | solution.py:64
  148.5 0.8 all-reduce.5.cloned.1.call-done
  149.3 0.0 copy-start.1
  149.3 29.6 %fusion.14 = bf16[8,64,1792]{2,1,0:T(8,128)(2,1)S(1)} fusion(bf16[8192,1792]{1,0:T(8,128)(2,1)} %param.15, f32[8,64,8192]{2,1,0:T(8,128)} %reshape.95, bf16[8,64,8192]{2,1,0:T(8,128)(2,1)} %all-reduce.5.cloned.1.call-done), kind=kOutput, calls=%fused_computation.13 | convolution fusion | flops 15062663168 | bytes 56360960 | tf_op jit(solution)/shard_map/sih,hf->sif/dot_general | solution.py:66
  179.0 48.6 %all_to_all.17 = bf16[8,64,1792]{2,1,0:T(8,128)(2,1)S(1)} all-to-all(bf16[8,64,1792]{2,1,0:T(8,128)(2,1)S(1)} %fusion.14), channel_id=1, replica_groups=mesh['replica'=2,'ep'=8,'tp'=2] {'ep'}, dimensions={0} | all-to-all | bytes 3670016 | tf_op jit(solution)/shard_map/all_to_all | solution.py:69
  227.6 1.3 fusion.20
  228.9 0.0 copy-done.1
  (5 shorter events, 0.0 us)
Async XLA Ops:
  6.5 25.9 %copy-start = (bf16[1792,64]{0,1:T(8,128)(2,1)S(1)}, bf16[1792,64]{0,1:T(8,128)(2,1)}, u32[]{:S(2)}) copy-start(bf16[1792,64]{0,1:T(8,128)(2,1)} %param.11) | copy-start | bytes 688132
  6.5 24.5 %all-reduce.3.cloned.1.call-start = ((), (), s32[]{:S(2)}) async-start(), calls=%async_computation.3 | async-start | bytes 917504 | tf_op jit(solution)/shard_map/psum | solution.py:25
  7.3 142.1 %all-reduce.5.cloned.1.call-start = ((), (), s32[]{:S(2)}) async-start(), calls=%async_computation.4 | async-start | bytes 16777216 | tf_op jit(solution)/shard_map/psum | solution.py:63
  149.3 79.6 %copy-start.1 = (bf16[1792,64]{0,1:T(8,128)(2,1)S(1)}, bf16[1792,64]{0,1:T(8,128)(2,1)}, u32[]{:S(2)}) copy-start(bf16[1792,64]{0,1:T(8,128)(2,1)} %param.11) | copy-start | bytes 688132
Sparse Core Ops, SparseCore 0:
  9.7 21.2 all-reduce.2
  111.4 37.8 all-reduce.4
where the time goes:
time: 237 us; the launch traced here: 236 us
  blocking collectives  111 us (47%)
  matrix products  56.3 us (24%)
  local copies, waits for them, and re-layouts  28.6 us (12%)
  waiting for transfers between devices  23.7 us (10%)
  between operations  13.5 us (6%)
  other arithmetic  2.93 us (1%)
    all_to_all x1, blocking collectives, on_device(): lax.all_to_all(result, 'ep', split_axis=0, concat_axis=0, tiled=True)  48.6 us
    all_to_all x1, blocking collectives, on_device(): lax.all_to_all(send_rows, 'ep', split_axis=0, concat_axis=0, tiled=True)  48.6 us
    dot_general x1, matrix products, on_device(): jnp.einsum('sih,hf->sif', gated, down_weight, preferred_element_type=jnp....  29.6 us
    dot_general x1, matrix products, on_device(): jnp.einsum('sif,fh->sih', rows_in, up_weight, preferred_element_type=jnp....  22.7 us
    psum x1, waiting for transfers between devices, on_device(): lax.psum(dense_mine.astype(jnp.bfloat16), 'tp').astype(jnp.float32)  22.1 us
    reshape x1, local copies, waits for them, and re-layouts, on_device(): column_gate = jnp.repeat(gates_in, span, axis=2)  19 us
    all_to_all x1, blocking collectives, on_device(): lax.all_to_all(send_gates.astype(jnp.bfloat16), 'ep', split_axis=0, conca...  9.95 us
    broadcast_in_dim x1, local copies, waits for them, and re-layouts, on_device(): column_gate = jnp.repeat(gates_in, span, axis=2)  7.61 us
  transfers between devices with their start and end apart: 2, of which 2 were waited for; matrix products, arithmetic and copies ran while one was open for 12% of the time, Pallas kernels for 0%

commit v1 on v0

v1 whole, which is shorter than its diff:
```python
import functools

import jax
import jax.numpy as jnp
from jax import lax
from jax.experimental import pallas as pl
from jax.experimental.pallas import tpu as pltpu
from jax.sharding import PartitionSpec as P

FF_E = 1024
CAP = 12
RING = 8
UP_BUFS = 4
MESH = pl.DeviceIdType.MESH
F32 = jnp.float32
BF16 = jnp.bfloat16


def nt_dot(a, b):
    return lax.dot_general(a, b, (((1,), (1,)), ((), ())), preferred_element_type=F32)


def dot(a, b):
    return jnp.dot(a, b, preferred_element_type=F32)


def ring_device(pos):
    back = pos // (RING // 2)
    return (1 - back) * 2 * pos + back * (2 * (RING - 1 - pos) + 1)


def expert_kernel(
    slots, rows_ref, up_ref, down_ref, out_ref, gather, xy, pre_own, pre_peer, sel, sel_t, gate_col,
    send_buf, recv_buf, up_buf, down_buf, up_sem, down_sem, g_send, g_recv, p_send, p_recv, r_send, r_recv,
):
    tok, width_ext = rows_ref.shape
    width = down_buf.shape[2]
    span = FF_E
    cap = CAP * RING
    total_rows = slots * cap
    tokens = tok * RING
    half = tok // 2

    ep = lax.axis_index("ep")
    tp = lax.axis_index("tp")
    x_pos = lax.rem(ep, 2)
    z_pos = ep // 2
    pos = z_pos + x_pos * (RING - 1 - 2 * z_pos)
    right = ring_device(lax.rem(pos + 1, RING))
    left = ring_device(lax.rem(pos + RING - 1, RING))
    sides = (right, left)
    step_of = (1, -1)

    def up_copy(s):
        b = lax.rem(s, UP_BUFS)
        return pltpu.make_async_copy(
            up_ref.at[:, pl.ds(pl.multiple_of(s * span, span), span)], up_buf.at[b], up_sem.at[b]
        )

    def down_copy(s):
        return pltpu.make_async_copy(
            down_ref.at[pl.ds(pl.multiple_of(s * span, span), span), :], down_buf.at[s], down_sem.at[s]
        )

    barrier = pltpu.get_barrier_semaphore()
    for side in sides:
        pl.semaphore_signal(barrier, inc=1, device_id={"ep": side}, device_id_type=MESH)
    pl.semaphore_signal(barrier, inc=1, device_id={"tp": 1 - tp}, device_id_type=MESH)
    gather[pos] = rows_ref[...]
    pl.semaphore_wait(barrier, 3)

    def gather_copy(way, k):
        block = lax.rem(pos - step_of[way] * k + RING, RING)
        if k == RING // 2 - 1:
            ref = gather.at[block, pl.ds(way * half, half), :]
        else:
            ref = gather.at[block]
        return pltpu.make_async_remote_copy(
            src_ref=ref, dst_ref=ref, send_sem=g_send.at[way, k], recv_sem=g_recv.at[way, k],
            device_id={"ep": sides[way]}, device_id_type=MESH,
        )

    steps = RING // 2
    copies = [[None] * steps, [None] * steps]
    for k in range(steps):
        for way in range(2):
            if k:
                copies[way][k - 1].wait_recv()
            copies[way][k] = gather_copy(way, k)
            copies[way][k].start()
        if k == 0:
            for s in range(UP_BUFS):
                up_copy(s).start()
            for s in range(slots):
                down_copy(s).start()
    for way in range(2):
        copies[way][steps - 1].wait_recv()
    for way in range(2):
        for k in range(steps):
            copies[way][k].wait_send()

    gates = gather[:, :, width:].reshape(tokens, width_ext - width)
    experts = (width_ext - width) // 2
    first = ep * slots
    lane = lax.broadcasted_iota(jnp.int32, (2 * experts, 128), 0)
    slot = lax.broadcasted_iota(jnp.int32, (2 * experts, 128), 1)
    inside = slot < slots
    pick_hi = ((lane == slot + first) & inside).astype(BF16)
    pick_lo = ((lane == slot + first + experts) & inside).astype(BF16)
    gate_hi = dot(gates, pick_hi).astype(BF16)
    gate_lo = dot(gates, pick_lo).astype(BF16)
    lane_t = lax.broadcasted_iota(jnp.int32, (16, 2 * experts), 1)
    slot_t = lax.broadcasted_iota(jnp.int32, (16, 2 * experts), 0)
    pick_t = ((lane_t == slot_t + first) & (slot_t < slots)).astype(BF16)
    need_t = nt_dot(pick_t, gates) > 0.0
    need = gate_hi.astype(F32) > 0.0
    t_row = lax.broadcasted_iota(jnp.int32, (tokens, tokens), 0)
    t_col = lax.broadcasted_iota(jnp.int32, (tokens, tokens), 1)
    lower = (t_col <= t_row).astype(F32).astype(BF16)
    upper = (t_row <= t_col).astype(F32).astype(BF16)
    order = dot(lower, need.astype(F32).astype(BF16))
    order_t = dot(need_t.astype(F32).astype(BF16), upper)
    order = jnp.where(need, order, 0.0).astype(BF16)
    order_t = jnp.where(need_t, order_t, 0.0).astype(BF16)

    def place_of(shape, dim):
        j = lax.broadcasted_iota(jnp.int32, shape, dim)
        c = j
        for s in range(1, slots):
            c = c - jnp.where(j >= s * cap, cap, 0)
        return (c + 1).astype(F32)

    def spread(shape, dim):
        j = lax.broadcasted_iota(jnp.int32, shape, dim)
        s = lax.broadcasted_iota(jnp.int32, shape, 1 - dim)
        return (j >= s * cap) & (j < (s + 1) * cap)

    spread_c = spread((128, total_rows), 1).astype(F32).astype(BF16)
    spread_r = spread((total_rows, 16), 0).astype(F32).astype(BF16)
    sel_t[...] = (dot(order, spread_c) == place_of((1, total_rows), 1)).astype(F32).astype(BF16)
    sel[...] = (dot(spread_r, order_t) == place_of((total_rows, 1), 0)).astype(F32).astype(BF16)
    row_gates = dot(sel[...], gate_hi) + dot(sel[...], gate_lo)
    own_slot = spread((total_rows, 128), 0)
    gate_col[...] = jnp.sum(jnp.where(own_slot, row_gates, 0.0), axis=1, keepdims=True)

    def peer_copy(s):
        return pltpu.make_async_remote_copy(
            src_ref=pre_own.at[s], dst_ref=pre_peer.at[s], send_sem=p_send.at[s], recv_sem=p_recv.at[s],
            device_id={"tp": 1 - tp}, device_id_type=MESH,
        )

    def up_step(s, carry):
        at = pl.ds(pl.multiple_of(s * cap, cap), cap)
        all_rows = gather[:, :, :width].reshape(tokens, width)
        x = dot(sel[at, :], all_rows).astype(BF16)
        up_copy(s).wait()
        pre_own[s] = dot(x, up_buf[lax.rem(s, UP_BUFS)]).astype(BF16)
        peer_copy(s).start()

        @pl.when(s + UP_BUFS < slots)
        def _():
            up_copy(s + UP_BUFS).start()

        return carry

    lax.fori_loop(0, slots, up_step, 0)

    def down_step(s, carry):
        at = pl.ds(pl.multiple_of(s * cap, cap), cap)
        peer_copy(s).wait()
        pre = pre_own[s].astype(F32) + pre_peer[s].astype(F32)
        gated = (jax.nn.silu(pre) * gate_col[at, :]).astype(BF16)
        down_copy(s).wait()
        xy[at, :] = dot(gated, down_buf[s]).astype(BF16)
        return carry

    lax.fori_loop(0, slots, down_step, 0)

    def chunk(dest, start, rows):
        at = pl.ds(pl.multiple_of(dest * tok + start, half), rows)
        return dot(sel_t[at, :], xy[...])

    def reduce_copy(way, k):
        at = pl.ds(way * half, half) if k == 0 else pl.ds(0, tok)
        return pltpu.make_async_remote_copy(
            src_ref=send_buf.at[way, k, at, :], dst_ref=recv_buf.at[way, k, at, :],
            send_sem=r_send.at[way, k], recv_sem=r_recv.at[way, k],
            device_id={"ep": sides[way]}, device_id_type=MESH,
        )

    for k in range(steps):
        for way in range(2):
            dest = lax.rem(pos + step_of[way] * (steps - k) + RING, RING)
            if k == 0:
                own = chunk(dest, way * half, half)
                send_buf[way, k, pl.ds(way * half, half), :] = own.astype(BF16)
            else:
                own = chunk(dest, 0, tok)
                reduce_copy(way, k - 1).wait_recv()
                if k == 1:
                    at = slice(way * half, (way + 1) * half)
                    other = slice((1 - way) * half, (2 - way) * half)
                    send_buf[way, k, other, :] = own[other].astype(BF16)
                    send_buf[way, k, at, :] = (own[at] + recv_buf[way, 0, at, :].astype(F32)).astype(BF16)
                else:
                    send_buf[way, k] = (own + recv_buf[way, k - 1].astype(F32)).astype(BF16)
            reduce_copy(way, k).start()
    own = chunk(pos, 0, tok)
    for way in range(2):
        reduce_copy(way, steps - 1).wait_recv()
        own = own + recv_buf[way, steps - 1].astype(F32)
    out_ref[...] = own
    for way in range(2):
        for k in range(steps):
            reduce_copy(way, k).wait_send()


def experts_on_ring(rows_ext, up_weight, down_weight):
    tok, width_ext = rows_ext.shape
    width = up_weight.shape[0]
    slots = up_weight.shape[1] // FF_E
    cap = CAP * RING
    steps = RING // 2
    vmem = pl.BlockSpec(memory_space=pltpu.VMEM)
    hbm = pl.BlockSpec(memory_space=pl.ANY)
    dma = pltpu.SemaphoreType.DMA
    return pl.pallas_call(
        functools.partial(expert_kernel, slots),
        out_shape=jax.ShapeDtypeStruct((tok, width), F32),
        in_specs=[vmem, hbm, hbm],
        out_specs=vmem,
        scratch_shapes=[
            pltpu.VMEM((RING, tok, width_ext), BF16),
            pltpu.VMEM((slots * cap, width), BF16),
            pltpu.VMEM((slots, cap, FF_E), BF16),
            pltpu.VMEM((slots, cap, FF_E), BF16),
            pltpu.VMEM((slots * cap, RING * tok), BF16),
            pltpu.VMEM((RING * tok, slots * cap), BF16),
            pltpu.VMEM((slots * cap, 1), F32),
            pltpu.VMEM((2, steps, tok, width), BF16),
            pltpu.VMEM((2, steps, tok, width), BF16),
            pltpu.VMEM((UP_BUFS, width, FF_E), BF16),
            pltpu.VMEM((slots, FF_E, width), BF16),
            dma((UP_BUFS,)),
            dma((slots,)),
            dma((2, steps)),
            dma((2, steps)),
            dma((slots,)),
            dma((slots,)),
            dma((2, steps)),
            dma((2, steps)),
        ],
        compiler_params=pltpu.CompilerParams(
            collective_id=0, has_side_effects=True, vmem_limit_bytes=62 * 1024 * 1024
        ),
    )(rows_ext, up_weight, down_weight)


def experts_by_exchange(normed_half, slot_gate, up_weight, down_weight):
    columns = up_weight.shape[1]
    tok_rows = normed_half.shape[0]
    experts = slot_gate.shape[1]
    peers = lax.axis_size("ep")
    local_slots = max(1, columns // FF_E)
    span = min(FF_E, columns)
    capacity = min(tok_rows, CAP * local_slots)
    expert_ids = jnp.arange(experts, dtype=jnp.int32)
    peer_ids = jnp.arange(peers, dtype=jnp.int32)
    slot_of_peer = (
        peer_ids[:, None] * columns // FF_E + jnp.arange(local_slots, dtype=jnp.int32)[None, :]
    )
    pick_table = (slot_of_peer[:, :, None] == expert_ids[None, None, :]).astype(F32)
    peer_gates = jnp.einsum("ts,pls->tpl", slot_gate, pick_table, precision=lax.Precision.HIGHEST)
    need = (jnp.sum(peer_gates, axis=-1) > 0.0).astype(jnp.int32)
    position = jnp.cumsum(need, axis=0) - 1
    slot_pos = jnp.arange(capacity, dtype=jnp.int32)
    selector = (need.T[:, None, :] == 1) & (position.T[:, None, :] == slot_pos[None, :, None])
    select_b = selector.astype(BF16)
    send_gates = jnp.einsum(
        "pct,tpl->pcl", selector.astype(F32), peer_gates, precision=lax.Precision.HIGHEST
    )
    send_rows = jnp.einsum(
        "pct,tf->pcf", select_b, normed_half.astype(BF16), preferred_element_type=F32
    ).astype(BF16)
    rows_in = lax.all_to_all(send_rows, "ep", split_axis=0, concat_axis=0, tiled=True)
    gates_in = lax.all_to_all(
        send_gates.astype(BF16), "ep", split_axis=0, concat_axis=0, tiled=True
    ).astype(F32)
    part_pre = jnp.einsum("sif,fh->sih", rows_in, up_weight, preferred_element_type=F32)
    pre = lax.psum(part_pre.astype(BF16), "tp").astype(F32)
    column_gate = jnp.repeat(gates_in, span, axis=2)
    gated = (jax.nn.silu(pre) * column_gate).astype(BF16)
    result = jnp.einsum("sih,hf->sif", gated, down_weight, preferred_element_type=F32).astype(BF16)
    returned = lax.all_to_all(result, "ep", split_axis=0, concat_axis=0, tiled=True)
    return jnp.einsum("pct,pcf->tf", select_b, returned, preferred_element_type=F32)


def on_device(
    ring, residual_in, dense_terms, norm_gain, router_weight, routes, placement, up_weight, down_weight
):
    half_width = up_weight.shape[0]
    experts = placement.shape[0]
    full_width = residual_in.shape[1]
    tp = lax.axis_index("tp")
    start = tp * half_width
    other = (1 - tp) * half_width

    def cut(a, at):
        return lax.dynamic_slice_in_dim(a, at, half_width, a.ndim - 1)

    theirs = lax.ppermute(cut(dense_terms[0], other), "tp", [(0, 1), (1, 0)])
    state_half = cut(residual_in, start).astype(F32) + (
        cut(dense_terms[0], start).astype(F32) + theirs.astype(F32)
    )
    scaled = state_half * cut(norm_gain, start)
    part_logits = jnp.dot(scaled, router_weight.astype(F32), precision=lax.Precision.HIGHEST)
    part_sq = jnp.sum(state_half * state_half, axis=-1, keepdims=True)
    sums = lax.psum(jnp.concatenate([part_logits, part_sq], axis=1), "tp")
    scale = lax.rsqrt(sums[:, experts:] / full_width + 1e-06)
    scores = jax.nn.sigmoid(sums[:, :experts] * scale)
    normed_half = scaled * scale
    expert_ids = jnp.arange(experts, dtype=jnp.int32)
    routed = jnp.any(routes[:, :, None] == expert_ids[None, None, :], axis=1)
    chosen = jnp.where(routed, scores, 0.0)
    expert_gate = 2.827 * chosen / jnp.sum(chosen, axis=-1, keepdims=True)
    slot_table = (placement[:, None] == expert_ids[None, :]).astype(F32)
    slot_gate = jnp.dot(expert_gate, slot_table, precision=lax.Precision.HIGHEST)
    if ring:
        gate_hi = slot_gate.astype(BF16)
        gate_lo = (slot_gate - gate_hi.astype(F32)).astype(BF16)
        rows_ext = jnp.concatenate([normed_half.astype(BF16), gate_hi, gate_lo], axis=1)
        expert_sum = experts_on_ring(rows_ext, up_weight, down_weight)
    else:
        expert_sum = experts_by_exchange(normed_half, slot_gate, up_weight, down_weight)
    return (state_half + expert_sum).astype(BF16)


def solution(mesh):
    ring = mesh.shape["ep"] == RING
    in_specs = (
        P(("replica", "ep"), None),
        P("tp", ("replica", "ep"), None),
        P(),
        P("tp", None),
        P(("replica", "ep"), None),
        P(),
        P("tp", "ep"),
        P("ep", "tp"),
    )
    out_specs = P(("replica", "ep"), "tp")
    return jax.shard_map(
        functools.partial(on_device, ring), mesh=mesh, in_specs=in_specs, out_specs=out_specs, check_vma=False
    )
```

time: 237 us -> 89.7 us (0.38)
  blocking collectives: 111 us -> 3.4 us
  Pallas kernels: 0 us -> 74.6 us
  matrix products: 56.3 us -> 2.35 us
  local copies, waits for them, and re-layouts: 28.6 us -> 3.44 us
  waiting for transfers between devices: 23.7 us -> 0.01 us
  between operations: 13.5 us -> 0.08 us
    all_to_all x3 -> x0, blocking collectives: 107 us -> none  [the longest x1 48.6 us: on_device(): lax.all_to_all(result, 'ep', split_axis=0, concat_axis=0, tiled=True)]
    pallas_call x0 -> x1, Pallas kernels: none -> 74.6 us  [experts_on_ring(): pl.pallas_call(functools.partial(expert_kernel, slots), out_shape=jax.Sha...]
    dot_general x7 -> x1, matrix products: 55.5 us -> 1.46 us  [on_device(): jnp.dot(scaled, router_weight.astype(F32), precision=lax.Precision.HIGHEST)]
    psum x2 -> x0, waiting for transfers between devices: 22.9 us -> none  [the longest x1 22.1 us: on_device(): lax.psum(dense_mine.astype(jnp.bfloat16), 'tp').astype(jnp.float32)]
    reshape x1 -> x0, local copies, waits for them, and re-layouts: 19 us -> none  [on_device(): column_gate = jnp.repeat(gates_in, span, axis=2)]
    broadcast_in_dim x1, local copies, waits for them, and re-layouts: 7.61 us -> 0.1 us  [on_device(): part_sq = jnp.sum(state_half * state_half, axis=-1, keepdims=True)]
    convert_element_type x0 -> x2, other arithmetic: none -> 2.99 us  [the longest x1 1.81 us: on_device(): return (state_half + expert_sum).astype(BF16)]
  transfers between devices with their start and end apart: 2 -> 1, of which waited for: 2 -> 0; matrix products, arithmetic and copies ran while one was open for 12% -> 2% of each run, Pallas kernels for 0% -> 0%
where the time goes in v1:
time: 89.7 us; the launch traced here: 89.3 us
  Pallas kernels  74.6 us (83%)
  other arithmetic  4.88 us (5%)
  local copies, waits for them, and re-layouts  3.44 us (4%)
  blocking collectives  3.4 us (4%)
  matrix products  2.35 us (3%)
    pallas_call x1, Pallas kernels, experts_on_ring(): pl.pallas_call(functools.partial(expert_kernel, slots), out_shape=jax.Sha...  74.6 us
    psum x1, blocking collectives, on_device(): sums = lax.psum(jnp.concatenate([part_logits, part_sq], axis=1), 'tp')  3.4 us
    convert_element_type x1, other arithmetic, on_device(): return (state_half + expert_sum).astype(BF16)  1.81 us
  transfers between devices with their start and end apart: 1, of which 0 were waited for; matrix products, arithmetic and copies ran while one was open for 2% of the time, Pallas kernels for 0%

profile of v1, /device:TPU:0, one launch (start us, length us, event | category | flops | bytes accessed | tf_op | source)
XLA Modules:
  0.0 89.3 jit_solution(7638826290214442226)
XLA Ops:
  0.0 0.0 copy-start
  0.0 1.0 %dynamic-slice_bitcast_fusion = bf16[64,1792]{1,0:T(8,128)(2,1)S(1)} fusion(bf16[1,64,3584]{2,1,0:T(8,128)(2,1)} %param.9, s32[]{:T(128)S(6)} %select_n.13), kind=kLoop, calls=%fused_computation.10 | loop fusion | bytes 458756 | tf_op jit(solution)/shard_map/dynamic_slice | solution.py:309
  1.0 0.5 collective-permute-start
  1.5 0.8 copy.14
  2.3 0.8 dynamic_slice.18
  3.1 0.2 fusion.3
  3.2 0.0 collective-permute-done
  3.3 1.3 %multiply_reduce_fusion = f32[64]{0:T(128)S(1)} fusion(bf16[64,1792]{1,0:T(8,128)(2,1)S(1)} %collective-permute-done, bf16[1,64,3584]{2,1,0:T(8,128)(2,1)} %param.9, s32[]{:T(128)S(6)} %select_n.12, bf16[64,3584]{1,0:T(8,128)(2,1)} %param.8), kind=kLoop, calls=%fused_computation.4 | loop fusion | flops 802752 | bytes 688388 | tf_op jit(solution)/shard_map/reduce_sum | solution.py:317
  4.5 0.1 copy.13
  4.6 0.0 copy-done
  4.6 1.5 %fusion.1 = f32[64,64]{1,0:T(8,128)S(1)} fusion(bf16[1792,64]{0,1:T(8,128)(2,1)S(1)} %copy-done, f32[1792]{0:T(1024)S(1)} %dynamic_slice.18, bf16[64,1792]{1,0:T(8,128)(2,1)S(1)} %collective-permute-done, bf16[1,64,3584]{2,1,0:T(8,128)(2,1)} %param.9, s32[]{:T(128)S(6)} %select_n.12, bf16[64,3584]{1,0:T(8,128)(2,1)} %param.8), kind=kOutput, calls=%fused_computation.5 | convolution fusion | flops 88768512 | bytes 941060 | tf_op jit(solution)/shard_map/dot_general | solution.py:316
  6.1 0.1 pad_maximum_fusion
  6.2 3.4 %psum.7 = f32[64,65]{1,0:T(8,128)S(1)} all-reduce(f32[64,65]{1,0:T(8,128)S(1)} %pad_maximum_fusion), channel_id=1, replica_groups=mesh['replica'=2,'ep'=8,'tp'=2] {'tp'}, use_global_device_ids=true, to_apply=%region_1.0 | all-reduce | flops 4160 | bytes 33280 | tf_op jit(solution)/shard_map/psum | solution.py:318
  9.6 0.2 fusion.12
  9.8 0.2 fusion.20
  10.0 0.9 %subtract_convert_fusion = (bf16[64,64]{1,0:T(8,128)(2,1)S(1)}, bf16[64,64]{1,0:T(8,128)(2,1)S(1)}) fusion(s32[64]{0:T(128)} %param.13, f32[64]{0:T(128)S(1)} %fusion.20, pred[64,64]{1,0:T(8,128)(4,1)S(1)} %fusion.3, f32[64]{0:T(128)S(1)} %fusion.12, f32[64,65]{1,0:T(8,128)S(1)} %psum.7), kind=kOutput, calls=%fused_computation.22 | convolution fusion | flops 3194880 | bytes 37888 | tf_op jit(solution)/shard_map/dot_general | solution.py:327
  10.9 1.2 %multiply_convert_fusion = bf16[64,1792]{1,0:T(8,128)(2,1)S(1)} fusion(f32[64]{0:T(128)S(1)} %fusion.12, f32[1792]{0:T(1024)S(1)} %dynamic_slice.18, bf16[64,1792]{1,0:T(8,128)(2,1)S(1)} %collective-permute-done, bf16[1,64,3584]{2,1,0:T(8,128)(2,1)} %param.9, s32[]{:T(128)S(6)} %select_n.12, bf16[64,3584]{1,0:T(8,128)(2,1)} %param.8), kind=kLoop, calls=%fused_computation.3 | loop fusion | flops 917504 | bytes 924932 | tf_op jit(solution)/shard_map/convert_element_type | solution.py:331
  12.0 0.8 concatenate.7.rows_ref
  12.8 0.0 copy-start.1
  12.8 0.0 copy-start.2
  12.8 74.6 %shard_map.82 = f32[64,1792]{1,0:T(8,128)} custom-call(bf16[64,1920]{1,0:T(8,128)(2,1)} %concatenate.7.rows_ref, bf16[1792,8192]{1,0:T(8,128)(2,1)} %up_ref.1, bf16[8192,1792]{1,0:T(8,128)(2,1)} %down_ref.1), custom_call_target="tpu_custom_call" | custom-call | tf_op jit(solution)/shard_map/pallas_call | solution.py:227
  87.5 0.0 copy-done.1
  87.5 0.0 copy-done.2
  87.5 1.8 %add_convert_fusion = bf16[64,1792]{1,0:T(8,128)(2,1)} fusion(f32[64,1792]{1,0:T(8,128)} %shard_map.82, bf16[64,1792]{1,0:T(8,128)(2,1)S(1)} %collective-permute-done, bf16[1,64,3584]{2,1,0:T(8,128)(2,1)S(1)} %copy-done.1, s32[]{:T(128)S(6)} %select_n.12, bf16[64,3584]{1,0:T(8,128)(2,1)S(1)} %copy-done.2), kind=kLoop, calls=%fused_computation.2 | loop fusion | flops 802816 | bytes 1376260 | tf_op jit(solution)/shard_map/convert_element_type | solution.py:335
Async XLA Ops:
  0.0 4.6 %copy-start = (bf16[1792,64]{0,1:T(8,128)(2,1)S(1)}, bf16[1792,64]{0,1:T(8,128)(2,1)}, u32[]{:S(2)}) copy-start(bf16[1792,64]{0,1:T(8,128)(2,1)} %param.11) | copy-start | bytes 688132
  1.0 2.2 %collective-permute-start = (bf16[64,1792]{1,0:T(8,128)(2,1)S(1)}, bf16[64,1792]{1,0:T(8,128)(2,1)S(1)}, u32[]{:S(2)}, u32[]{:S(2)}) collective-permute-start(bf16[64,1792]{1,0:T(8,128)(2,1)S(1)} %dynamic-slice_bitcast_fusion), channel_id=1, source_target_pairs={{0,1},{1,0},{2,3},{3,2},{4,5},{5,4},{6,7},{7,6},{8,9},{9,8},{10,11... | collective-permute-start | bytes 688136 | tf_op jit(solution)/shard_map/ppermute | solution.py:311
  12.8 74.6 %copy-start.1 = (bf16[1,64,3584]{2,1,0:T(8,128)(2,1)S(1)}, bf16[1,64,3584]{2,1,0:T(8,128)(2,1)}, u32[]{:S(2)}) copy-start(bf16[1,64,3584]{2,1,0:T(8,128)(2,1)} %param.9) | copy-start | bytes 1376260
  12.8 74.6 %copy-start.2 = (bf16[64,3584]{1,0:T(8,128)(2,1)S(1)}, bf16[64,3584]{1,0:T(8,128)(2,1)}, u32[]{:S(2)}) copy-start(bf16[64,3584]{1,0:T(8,128)(2,1)} %param.8) | copy-start | bytes 1376260

commit v2 on v1

--- a/solution.py
+++ b/solution.py
@@ -10,7 +10,9 @@
 FF_E = 1024
 CAP = 12
 RING = 8
-UP_BUFS = 4
+UP_BUFS = 6
+DOWN_BUFS = 12
+PARTS = 2
 MESH = pl.DeviceIdType.MESH
 F32 = jnp.float32
 BF16 = jnp.bfloat16
@@ -34,7 +36,8 @@
     send_buf, recv_buf, up_buf, down_buf, up_sem, down_sem, g_send, g_recv, p_send, p_recv, r_send, r_recv,
 ):
     tok, width_ext = rows_ref.shape
-    width = down_buf.shape[2]
+    part_w = down_buf.shape[2]
+    width = part_w * PARTS
     span = FF_E
     cap = CAP * RING
     total_rows = slots * cap
@@ -57,9 +60,17 @@
             up_ref.at[:, pl.ds(pl.multiple_of(s * span, span), span)], up_buf.at[b], up_sem.at[b]
         )
 
-    def down_copy(s):
+    def down_copy(j):
+        part = j // slots
+        s = j - part * slots
+        b = lax.rem(j, DOWN_BUFS)
         return pltpu.make_async_copy(
-            down_ref.at[pl.ds(pl.multiple_of(s * span, span), span), :], down_buf.at[s], down_sem.at[s]
+            down_ref.at[
+                pl.ds(pl.multiple_of(s * span, span), span),
+                pl.ds(pl.multiple_of(part * part_w, part_w), part_w),
+            ],
+            down_buf.at[b],
+            down_sem.at[b],
         )
 
     barrier = pltpu.get_barrier_semaphore()
@@ -69,35 +80,35 @@
     gather[pos] = rows_ref[...]
     pl.semaphore_wait(barrier, 3)
 
-    def gather_copy(way, k):
+    def gather_copy(way, k, c):
         block = lax.rem(pos - step_of[way] * k + RING, RING)
-        if k == RING // 2 - 1:
-            ref = gather.at[block, pl.ds(way * half, half), :]
-        else:
-            ref = gather.at[block]
+        ref = gather.at[block, pl.ds(c * half, half), :]
         return pltpu.make_async_remote_copy(
-            src_ref=ref, dst_ref=ref, send_sem=g_send.at[way, k], recv_sem=g_recv.at[way, k],
+            src_ref=ref, dst_ref=ref, send_sem=g_send.at[way, k, c], recv_sem=g_recv.at[way, k, c],
             device_id={"ep": sides[way]}, device_id_type=MESH,
         )
 
     steps = RING // 2
-    copies = [[None] * steps, [None] * steps]
+    copies = {}
     for k in range(steps):
-        for way in range(2):
-            if k:
-                copies[way][k - 1].wait_recv()
-            copies[way][k] = gather_copy(way, k)
-            copies[way][k].start()
+        for c in range(PARTS):
+            for way in range(2):
+                part = way if c == 0 else 1 - way
+                if k:
+                    copies[way, k - 1, part].wait_recv()
+                if k == steps - 1 and part != way:
+                    continue
+                copies[way, k, part] = gather_copy(way, k, part)
+                copies[way, k, part].start()
         if k == 0:
             for s in range(UP_BUFS):
                 up_copy(s).start()
-            for s in range(slots):
-                down_copy(s).start()
+            for j in range(DOWN_BUFS):
+                down_copy(j).start()
     for way in range(2):
-        copies[way][steps - 1].wait_recv()
-    for way in range(2):
-        for k in range(steps):
-            copies[way][k].wait_send()
+        copies[way, steps - 1, way].wait_recv()
+    for copy in copies.values():
+        copy.wait_send()
 
     gates = gather[:, :, width:].reshape(tokens, width_ext - width)
     experts = (width_ext - width) // 2
@@ -149,12 +160,17 @@
             device_id={"tp": 1 - tp}, device_id_type=MESH,
         )
 
+    def pick_step(i, carry):
+        cols = pl.ds(pl.multiple_of(i * 256, 256), 256)
+        xy[:, cols] = dot(sel[...], gather[:, :, cols].reshape(tokens, 256)).astype(BF16)
+        return carry
+
+    lax.fori_loop(0, width // 256, pick_step, 0)
+
     def up_step(s, carry):
         at = pl.ds(pl.multiple_of(s * cap, cap), cap)
-        all_rows = gather[:, :, :width].reshape(tokens, width)
-        x = dot(sel[at, :], all_rows).astype(BF16)
         up_copy(s).wait()
-        pre_own[s] = dot(x, up_buf[lax.rem(s, UP_BUFS)]).astype(BF16)
+        pre_own[s] = dot(xy[at, :], up_buf[lax.rem(s, UP_BUFS)]).astype(BF16)
         peer_copy(s).start()
 
         @pl.when(s + UP_BUFS < slots)
@@ -165,54 +181,74 @@
 
     lax.fori_loop(0, slots, up_step, 0)
 
-    def down_step(s, carry):
+    def down_step(part, s, carry):
         at = pl.ds(pl.multiple_of(s * cap, cap), cap)
-        peer_copy(s).wait()
-        pre = pre_own[s].astype(F32) + pre_peer[s].astype(F32)
-        gated = (jax.nn.silu(pre) * gate_col[at, :]).astype(BF16)
-        down_copy(s).wait()
-        xy[at, :] = dot(gated, down_buf[s]).astype(BF16)
+        j = part * slots + s
+        if part == 0:
+            peer_copy(s).wait()
+            pre = pre_own[s].astype(F32) + pre_peer[s].astype(F32)
+            gated = (jax.nn.silu(pre) * gate_col[at, :]).astype(BF16)
+            pre_own[s] = gated
+        else:
+            gated = pre_own[s]
+        down_copy(j).wait()
+        cols = slice(part * part_w, (part + 1) * part_w)
+        xy[at, cols] = dot(gated, down_buf[lax.rem(j, DOWN_BUFS)]).astype(BF16)
+
+        @pl.when(j + DOWN_BUFS < PARTS * slots)
+        def _():
+            down_copy(j + DOWN_BUFS).start()
+
         return carry
 
-    lax.fori_loop(0, slots, down_step, 0)
-
-    def chunk(dest, start, rows):
+    def chunk(dest, start, rows, part):
         at = pl.ds(pl.multiple_of(dest * tok + start, half), rows)
-        return dot(sel_t[at, :], xy[...])
-
-    def reduce_copy(way, k):
+        return dot(sel_t[at, :], xy[:, part * part_w : (part + 1) * part_w])
+
+    def reduce_copy(way, k, part):
         at = pl.ds(way * half, half) if k == 0 else pl.ds(0, tok)
+        cols = pl.ds(part * part_w, part_w)
         return pltpu.make_async_remote_copy(
-            src_ref=send_buf.at[way, k, at, :], dst_ref=recv_buf.at[way, k, at, :],
-            send_sem=r_send.at[way, k], recv_sem=r_recv.at[way, k],
+            src_ref=send_buf.at[way, k, at, cols], dst_ref=recv_buf.at[way, k, at, cols],
+            send_sem=r_send.at[way, k, part], recv_sem=r_recv.at[way, k, part],
             device_id={"ep": sides[way]}, device_id_type=MESH,
         )
 
-    for k in range(steps):
+    for part in range(PARTS):
+        lax.fori_loop(0, slots, functools.partial(down_step, part), 0)
+        dest = lax.rem(pos + steps, RING)
+        cols = slice(part * part_w, (part + 1) * part_w)
         for way in range(2):
-            dest = lax.rem(pos + step_of[way] * (steps - k) + RING, RING)
-            if k == 0:
-                own = chunk(dest, way * half, half)
-                send_buf[way, k, pl.ds(way * half, half), :] = own.astype(BF16)
-            else:
-                own = chunk(dest, 0, tok)
-                reduce_copy(way, k - 1).wait_recv()
+            rows = slice(way * half, (way + 1) * half)
+            send_buf[way, 0, rows, cols] = chunk(dest, way * half, half, part).astype(BF16)
+            reduce_copy(way, 0, part).start()
+
+    for k in range(1, steps):
+        for part in range(PARTS):
+            cols = slice(part * part_w, (part + 1) * part_w)
+            for way in range(2):
+                dest = lax.rem(pos + step_of[way] * (steps - k) + RING, RING)
+                own = chunk(dest, 0, tok, part)
+                reduce_copy(way, k - 1, part).wait_recv()
                 if k == 1:
                     at = slice(way * half, (way + 1) * half)
                     other = slice((1 - way) * half, (2 - way) * half)
-                    send_buf[way, k, other, :] = own[other].astype(BF16)
-                    send_buf[way, k, at, :] = (own[at] + recv_buf[way, 0, at, :].astype(F32)).astype(BF16)
+                    send_buf[way, k, other, cols] = own[other].astype(BF16)
+                    send_buf[way, k, at, cols] = (own[at] + recv_buf[way, 0, at, cols].astype(F32)).astype(BF16)
                 else:
-                    send_buf[way, k] = (own + recv_buf[way, k - 1].astype(F32)).astype(BF16)
-            reduce_copy(way, k).start()
-    own = chunk(pos, 0, tok)
-    for way in range(2):
-        reduce_copy(way, steps - 1).wait_recv()
-        own = own + recv_buf[way, steps - 1].astype(F32)
-    out_ref[...] = own
+                    send_buf[way, k, :, cols] = (own + recv_buf[way, k - 1, :, cols].astype(F32)).astype(BF16)
+                reduce_copy(way, k, part).start()
+    for part in range(PARTS):
+        cols = slice(part * part_w, (part + 1) * part_w)
+        own = chunk(pos, 0, tok, part)
+        for way in range(2):
+            reduce_copy(way, steps - 1, part).wait_recv()
+            own = own + recv_buf[way, steps - 1, :, cols].astype(F32)
+        out_ref[:, cols] = own
     for way in range(2):
         for k in range(steps):
-            reduce_copy(way, k).wait_send()
+            for part in range(PARTS):
+                reduce_copy(way, k, part).wait_send()
 
 
 def experts_on_ring(rows_ext, up_weight, down_weight):
@@ -240,15 +276,15 @@
             pltpu.VMEM((2, steps, tok, width), BF16),
             pltpu.VMEM((2, steps, tok, width), BF16),
             pltpu.VMEM((UP_BUFS, width, FF_E), BF16),
-            pltpu.VMEM((slots, FF_E, width), BF16),
+            pltpu.VMEM((DOWN_BUFS, FF_E, width // PARTS), BF16),
             dma((UP_BUFS,)),
-            dma((slots,)),
-            dma((2, steps)),
-            dma((2, steps)),
+            dma((DOWN_BUFS,)),
+            dma((2, steps, PARTS)),
+            dma((2, steps, PARTS)),
             dma((slots,)),
             dma((slots,)),
-            dma((2, steps)),
-            dma((2, steps)),
+            dma((2, steps, PARTS)),
+            dma((2, steps, PARTS)),
         ],
         compiler_params=pltpu.CompilerParams(
             collective_id=0, has_side_effects=True, vmem_limit_bytes=62 * 1024 * 1024

time: 89.7 us -> 80.4 us (0.90)
  Pallas kernels: 74.6 us -> 65.4 us
    pallas_call x1, Pallas kernels: 74.6 us -> 65.4 us  [experts_on_ring(): pl.pallas_call(functools.partial(expert_kernel, slots), out_shape=jax.Sha...]
where the time goes in v2:
time: 80.4 us; the launch traced here: 80 us
  Pallas kernels  65.4 us (81%)
  other arithmetic  4.88 us (6%)
  local copies, waits for them, and re-layouts  3.44 us (4%)
  blocking collectives  3.4 us (4%)
  matrix products  2.35 us (3%)
    pallas_call x1, Pallas kernels, experts_on_ring(): pl.pallas_call(functools.partial(expert_kernel, slots), out_shape=jax.Sha...  65.4 us
    psum x1, blocking collectives, on_device(): sums = lax.psum(jnp.concatenate([part_logits, part_sq], axis=1), 'tp')  3.4 us
    convert_element_type x1, other arithmetic, on_device(): return (state_half + expert_sum).astype(BF16)  1.81 us
    dynamic_slice x2, local copies, waits for them, and re-layouts, cut(): return lax.dynamic_slice_in_dim(a, at, half_width, a.ndim - 1)  1.77 us
  transfers between devices with their start and end apart: 1, of which 0 were waited for; matrix products, arithmetic and copies ran while one was open for 2% of the time, Pallas kernels for 0%

profile of v2, /device:TPU:0, one launch (start us, length us, event | category | flops | bytes accessed | tf_op | source)
XLA Modules:
  0.0 80.0 jit_solution(13272518319324577407)
XLA Ops:
  0.0 0.0 copy-start
  0.0 1.0 %dynamic-slice_bitcast_fusion = bf16[64,1792]{1,0:T(8,128)(2,1)S(1)} fusion(bf16[1,64,3584]{2,1,0:T(8,128)(2,1)} %param.9, s32[]{:T(128)S(6)} %select_n.13), kind=kLoop, calls=%fused_computation.10 | loop fusion | bytes 458756 | tf_op jit(solution)/shard_map/dynamic_slice | solution.py:345
  1.0 0.5 collective-permute-start
  1.5 0.8 copy.14
  2.3 0.8 dynamic_slice.18
  3.1 0.2 fusion.3
  3.2 0.0 collective-permute-done
  3.3 1.3 %multiply_reduce_fusion = f32[64]{0:T(128)S(1)} fusion(bf16[64,1792]{1,0:T(8,128)(2,1)S(1)} %collective-permute-done, bf16[1,64,3584]{2,1,0:T(8,128)(2,1)} %param.9, s32[]{:T(128)S(6)} %select_n.12, bf16[64,3584]{1,0:T(8,128)(2,1)} %param.8), kind=kLoop, calls=%fused_computation.4 | loop fusion | flops 802752 | bytes 688388 | tf_op jit(solution)/shard_map/reduce_sum | solution.py:353
  4.5 0.1 copy.13
  4.6 0.0 copy-done
  4.6 1.5 %fusion.1 = f32[64,64]{1,0:T(8,128)S(1)} fusion(bf16[1792,64]{0,1:T(8,128)(2,1)S(1)} %copy-done, f32[1792]{0:T(1024)S(1)} %dynamic_slice.18, bf16[64,1792]{1,0:T(8,128)(2,1)S(1)} %collective-permute-done, bf16[1,64,3584]{2,1,0:T(8,128)(2,1)} %param.9, s32[]{:T(128)S(6)} %select_n.12, bf16[64,3584]{1,0:T(8,128)(2,1)} %param.8), kind=kOutput, calls=%fused_computation.5 | convolution fusion | flops 88768512 | bytes 941060 | tf_op jit(solution)/shard_map/dot_general | solution.py:352
  6.1 0.1 pad_maximum_fusion
  6.2 3.4 %psum.7 = f32[64,65]{1,0:T(8,128)S(1)} all-reduce(f32[64,65]{1,0:T(8,128)S(1)} %pad_maximum_fusion), channel_id=1, replica_groups=mesh['replica'=2,'ep'=8,'tp'=2] {'tp'}, use_global_device_ids=true, to_apply=%region_1.0 | all-reduce | flops 4160 | bytes 33280 | tf_op jit(solution)/shard_map/psum | solution.py:354
  9.6 0.2 fusion.12
  9.8 0.2 fusion.20
  10.0 0.9 %subtract_convert_fusion = (bf16[64,64]{1,0:T(8,128)(2,1)S(1)}, bf16[64,64]{1,0:T(8,128)(2,1)S(1)}) fusion(s32[64]{0:T(128)} %param.13, f32[64]{0:T(128)S(1)} %fusion.20, pred[64,64]{1,0:T(8,128)(4,1)S(1)} %fusion.3, f32[64]{0:T(128)S(1)} %fusion.12, f32[64,65]{1,0:T(8,128)S(1)} %psum.7), kind=kOutput, calls=%fused_computation.22 | convolution fusion | flops 3194880 | bytes 37888 | tf_op jit(solution)/shard_map/dot_general | solution.py:363
  10.9 1.2 %multiply_convert_fusion = bf16[64,1792]{1,0:T(8,128)(2,1)S(1)} fusion(f32[64]{0:T(128)S(1)} %fusion.12, f32[1792]{0:T(1024)S(1)} %dynamic_slice.18, bf16[64,1792]{1,0:T(8,128)(2,1)S(1)} %collective-permute-done, bf16[1,64,3584]{2,1,0:T(8,128)(2,1)} %param.9, s32[]{:T(128)S(6)} %select_n.12, bf16[64,3584]{1,0:T(8,128)(2,1)} %param.8), kind=kLoop, calls=%fused_computation.3 | loop fusion | flops 917504 | bytes 924932 | tf_op jit(solution)/shard_map/convert_element_type | solution.py:367
  12.0 0.8 concatenate.7.rows_ref
  12.8 0.0 copy-start.1
  12.8 0.0 copy-start.2
  12.8 65.4 %shard_map.82 = f32[64,1792]{1,0:T(8,128)} custom-call(bf16[64,1920]{1,0:T(8,128)(2,1)} %concatenate.7.rows_ref, bf16[1792,8192]{1,0:T(8,128)(2,1)} %up_ref.1, bf16[8192,1792]{1,0:T(8,128)(2,1)} %down_ref.1), custom_call_target="tpu_custom_call" | custom-call | tf_op jit(solution)/shard_map/pallas_call | solution.py:263
  78.2 0.0 copy-done.1
  78.2 0.0 copy-done.2
  78.2 1.8 %add_convert_fusion = bf16[64,1792]{1,0:T(8,128)(2,1)} fusion(f32[64,1792]{1,0:T(8,128)} %shard_map.82, bf16[64,1792]{1,0:T(8,128)(2,1)S(1)} %collective-permute-done, bf16[1,64,3584]{2,1,0:T(8,128)(2,1)S(1)} %copy-done.1, s32[]{:T(128)S(6)} %select_n.12, bf16[64,3584]{1,0:T(8,128)(2,1)S(1)} %copy-done.2), kind=kLoop, calls=%fused_computation.2 | loop fusion | flops 802816 | bytes 1376260 | tf_op jit(solution)/shard_map/convert_element_type | solution.py:371
Async XLA Ops:
  0.0 4.6 %copy-start = (bf16[1792,64]{0,1:T(8,128)(2,1)S(1)}, bf16[1792,64]{0,1:T(8,128)(2,1)}, u32[]{:S(2)}) copy-start(bf16[1792,64]{0,1:T(8,128)(2,1)} %param.11) | copy-start | bytes 688132
  1.0 2.2 %collective-permute-start = (bf16[64,1792]{1,0:T(8,128)(2,1)S(1)}, bf16[64,1792]{1,0:T(8,128)(2,1)S(1)}, u32[]{:S(2)}, u32[]{:S(2)}) collective-permute-start(bf16[64,1792]{1,0:T(8,128)(2,1)S(1)} %dynamic-slice_bitcast_fusion), channel_id=1, source_target_pairs={{0,1},{1,0},{2,3},{3,2},{4,5},{5,4},{6,7},{7,6},{8,9},{9,8},{10,11... | collective-permute-start | bytes 688136 | tf_op jit(solution)/shard_map/ppermute | solution.py:347
  12.8 65.4 %copy-start.1 = (bf16[1,64,3584]{2,1,0:T(8,128)(2,1)S(1)}, bf16[1,64,3584]{2,1,0:T(8,128)(2,1)}, u32[]{:S(2)}) copy-start(bf16[1,64,3584]{2,1,0:T(8,128)(2,1)} %param.9) | copy-start | bytes 1376260
  12.8 65.4 %copy-start.2 = (bf16[64,3584]{1,0:T(8,128)(2,1)S(1)}, bf16[64,3584]{1,0:T(8,128)(2,1)}, u32[]{:S(2)}) copy-start(bf16[64,3584]{1,0:T(8,128)(2,1)} %param.8) | copy-start | bytes 1376260

commit v3 on v2

--- a/solution.py
+++ b/solution.py
@@ -32,10 +32,13 @@
 
 
 def expert_kernel(
-    slots, rows_ref, up_ref, down_ref, out_ref, gather, xy, pre_own, pre_peer, sel, sel_t, gate_col,
+    slots, res_ref, dense_ref, gain_ref, router_ref, routes_ref, place_ref, up_ref, down_ref, out_ref,
+    theirs, state, stat_own, stat_peer, d_send, d_recv, gather, xy, pre_own, pre_peer, sel, sel_t, gate_col,
     send_buf, recv_buf, up_buf, down_buf, up_sem, down_sem, g_send, g_recv, p_send, p_recv, r_send, r_recv,
 ):
-    tok, width_ext = rows_ref.shape
+    tok, full_width = res_ref.shape
+    experts = router_ref.shape[1]
+    width_ext = gather.shape[2]
     part_w = down_buf.shape[2]
     width = part_w * PARTS
     span = FF_E
@@ -77,8 +80,52 @@
     for side in sides:
         pl.semaphore_signal(barrier, inc=1, device_id={"ep": side}, device_id_type=MESH)
     pl.semaphore_signal(barrier, inc=1, device_id={"tp": 1 - tp}, device_id_type=MESH)
-    gather[pos] = rows_ref[...]
+    for s in range(UP_BUFS):
+        up_copy(s).start()
+    for j in range(DOWN_BUFS):
+        down_copy(j).start()
     pl.semaphore_wait(barrier, 3)
+
+    mine = pl.ds(pl.multiple_of(tp * width, width), width)
+    other = pl.ds(pl.multiple_of((1 - tp) * width, width), width)
+    dense_copy = pltpu.make_async_remote_copy(
+        src_ref=dense_ref.at[0, :, other], dst_ref=theirs, send_sem=d_send.at[0], recv_sem=d_recv.at[0],
+        device_id={"tp": 1 - tp}, device_id_type=MESH,
+    )
+    dense_copy.start()
+    partial = res_ref[:, mine].astype(F32)
+    own_dense = dense_ref[0, :, mine].astype(F32)
+    dense_copy.wait()
+    total = partial + (own_dense + theirs[...].astype(F32))
+    state[...] = total
+    scaled = total * gain_ref[:, mine]
+    stat_own[:, :experts] = jnp.dot(
+        scaled, router_ref[...].astype(F32), precision=lax.Precision.HIGHEST, preferred_element_type=F32
+    )
+    square = jnp.sum(total * total, axis=1, keepdims=True)
+    stat_own[:, experts:] = jnp.broadcast_to(square, (tok, stat_own.shape[1] - experts))
+    stat_copy = pltpu.make_async_remote_copy(
+        src_ref=stat_own, dst_ref=stat_peer, send_sem=d_send.at[1], recv_sem=d_recv.at[1],
+        device_id={"tp": 1 - tp}, device_id_type=MESH,
+    )
+    stat_copy.start()
+    expert_id = lax.broadcasted_iota(jnp.int32, (tok, experts), 1)
+    routed = routes_ref[:, 0:1] == expert_id
+    for r in range(1, routes_ref.shape[1]):
+        routed = routed | (routes_ref[:, r : r + 1] == expert_id)
+    table = place_ref[...] == lax.broadcasted_iota(jnp.int32, (experts, experts), 0)
+    table = table.astype(F32).astype(BF16)
+    stat_copy.wait()
+    logits = stat_own[:, :experts] + stat_peer[:, :experts]
+    mean_sq = (stat_own[:, experts : experts + 1] + stat_peer[:, experts : experts + 1]) / full_width
+    scale = lax.rsqrt(mean_sq + 1e-06)
+    gather[pos, :, :width] = (state[...] * gain_ref[:, mine] * scale).astype(BF16)
+    chosen = jnp.where(routed, jax.nn.sigmoid(logits * scale), 0.0)
+    gate = 2.827 * chosen / jnp.sum(chosen, axis=1, keepdims=True)
+    high = gate.astype(BF16)
+    low = (gate - high.astype(F32)).astype(BF16)
+    gather[pos, :, width : width + experts] = nt_dot(high, table).astype(BF16)
+    gather[pos, :, width + experts :] = nt_dot(low, table).astype(BF16)
 
     def gather_copy(way, k, c):
         block = lax.rem(pos - step_of[way] * k + RING, RING)
@@ -100,18 +147,12 @@
                     continue
                 copies[way, k, part] = gather_copy(way, k, part)
                 copies[way, k, part].start()
-        if k == 0:
-            for s in range(UP_BUFS):
-                up_copy(s).start()
-            for j in range(DOWN_BUFS):
-                down_copy(j).start()
     for way in range(2):
         copies[way, steps - 1, way].wait_recv()
     for copy in copies.values():
         copy.wait_send()
 
     gates = gather[:, :, width:].reshape(tokens, width_ext - width)
-    experts = (width_ext - width) // 2
     first = ep * slots
     lane = lax.broadcasted_iota(jnp.int32, (2 * experts, 128), 0)
     slot = lax.broadcasted_iota(jnp.int32, (2 * experts, 128), 1)
@@ -244,16 +285,20 @@
         for way in range(2):
             reduce_copy(way, steps - 1, part).wait_recv()
             own = own + recv_buf[way, steps - 1, :, cols].astype(F32)
-        out_ref[:, cols] = own
+        out_ref[:, cols] = (own + state[:, cols]).astype(out_ref.dtype)
     for way in range(2):
         for k in range(steps):
             for part in range(PARTS):
                 reduce_copy(way, k, part).wait_send()
 
 
-def experts_on_ring(rows_ext, up_weight, down_weight):
-    tok, width_ext = rows_ext.shape
+def block_on_ring(
+    residual_in, dense_terms, norm_gain, router_weight, routes, placement, up_weight, down_weight
+):
+    tok = residual_in.shape[0]
     width = up_weight.shape[0]
+    experts = placement.shape[0]
+    width_ext = width + 2 * experts
     slots = up_weight.shape[1] // FF_E
     cap = CAP * RING
     steps = RING // 2
@@ -262,10 +307,16 @@
     dma = pltpu.SemaphoreType.DMA
     return pl.pallas_call(
         functools.partial(expert_kernel, slots),
-        out_shape=jax.ShapeDtypeStruct((tok, width), F32),
-        in_specs=[vmem, hbm, hbm],
+        out_shape=jax.ShapeDtypeStruct((tok, width), BF16),
+        in_specs=[vmem] * 6 + [hbm, hbm],
         out_specs=vmem,
         scratch_shapes=[
+            pltpu.VMEM((tok, width), BF16),
+            pltpu.VMEM((tok, width), F32),
+            pltpu.VMEM((tok, 2 * experts), F32),
+            pltpu.VMEM((tok, 2 * experts), F32),
+            dma((2,)),
+            dma((2,)),
             pltpu.VMEM((RING, tok, width_ext), BF16),
             pltpu.VMEM((slots * cap, width), BF16),
             pltpu.VMEM((slots, cap, FF_E), BF16),
@@ -289,7 +340,9 @@
         compiler_params=pltpu.CompilerParams(
             collective_id=0, has_side_effects=True, vmem_limit_bytes=62 * 1024 * 1024
         ),
-    )(rows_ext, up_weight, down_weight)
+    )(
+        residual_in, dense_terms, norm_gain[None], router_weight, routes, placement[None], up_weight, down_weight
+    )
 
 
 def experts_by_exchange(normed_half, slot_gate, up_weight, down_weight):
@@ -334,6 +387,10 @@
 def on_device(
     ring, residual_in, dense_terms, norm_gain, router_weight, routes, placement, up_weight, down_weight
 ):
+    if ring:
+        return block_on_ring(
+            residual_in, dense_terms, norm_gain, router_weight, routes, placement, up_weight, down_weight
+        )
     half_width = up_weight.shape[0]
     experts = placement.shape[0]
     full_width = residual_in.shape[1]
@@ -361,13 +418,7 @@
     expert_gate = 2.827 * chosen / jnp.sum(chosen, axis=-1, keepdims=True)
     slot_table = (placement[:, None] == expert_ids[None, :]).astype(F32)
     slot_gate = jnp.dot(expert_gate, slot_table, precision=lax.Precision.HIGHEST)
-    if ring:
-        gate_hi = slot_gate.astype(BF16)
-        gate_lo = (slot_gate - gate_hi.astype(F32)).astype(BF16)
-        rows_ext = jnp.concatenate([normed_half.astype(BF16), gate_hi, gate_lo], axis=1)
-        expert_sum = experts_on_ring(rows_ext, up_weight, down_weight)
-    else:
-        expert_sum = experts_by_exchange(normed_half, slot_gate, up_weight, down_weight)
+    expert_sum = experts_by_exchange(normed_half, slot_gate, up_weight, down_weight)
     return (state_half + expert_sum).astype(BF16)
 
 

time: 80.4 us -> 75.6 us (0.940)
  other arithmetic: 4.88 us -> 0 us
  Pallas kernels: 65.4 us -> 69 us
  blocking collectives: 3.4 us -> 0 us
  local copies, waits for them, and re-layouts: 3.44 us -> 6.27 us
  matrix products: 2.35 us -> 0 us
    unnamed x7 -> x3, local copies, waits for them, and re-layouts: 0.78 us -> 4.94 us
    pallas_call x1, Pallas kernels: 65.4 us -> 69 us  [block_on_ring(): pl.pallas_call(functools.partial(expert_kernel, slots), out_shape=jax.Sha...]
    psum x1 -> x0, blocking collectives: 3.4 us -> none  [on_device(): sums = lax.psum(jnp.concatenate([part_logits, part_sq], axis=1), 'tp')]
    convert_element_type x2 -> x0, other arithmetic: 2.99 us -> none  [the longest x1 1.81 us: on_device(): return (state_half + expert_sum).astype(BF16)]
    dot_general x2 -> x0, matrix products: 2.35 us -> none  [the longest x1 1.46 us: on_device(): jnp.dot(scaled, router_weight.astype(F32), precision=lax.Precision.HIGHEST)]
    dynamic_slice x2 -> x0, local copies, waits for them, and re-layouts: 1.77 us -> none  [cut(): return lax.dynamic_slice_in_dim(a, at, half_width, a.ndim - 1)]
    reduce_sum x2 -> x0, other arithmetic: 1.46 us -> none  [the longest x1 1.26 us: on_device(): part_sq = jnp.sum(state_half * state_half, axis=-1, keepdims=True)]
    broadcast_in_dim x1, local copies, waits for them, and re-layouts: 0.1 us -> 1.32 us  [block_on_ring(): norm_gain[None]]
  transfers between devices with their start and end apart: 1 -> 0, of which waited for: 0 -> 0; matrix products, arithmetic and copies ran while one was open for 2% -> 0% of each run, Pallas kernels for 0% -> 0%
where the time goes in v3:
time: 75.6 us; the launch traced here: 75.3 us
  Pallas kernels  69 us (91%)
  local copies, waits for them, and re-layouts  6.27 us (8%)
    pallas_call x1, Pallas kernels, block_on_ring(): pl.pallas_call(functools.partial(expert_kernel, slots), out_shape=jax.Sha...  69 us
    unnamed x3, local copies, waits for them, and re-layouts  4.94 us

profile of v3, /device:TPU:0, one launch (start us, length us, event | category | flops | bytes accessed | tf_op | source)
XLA Modules:
  0.0 75.3 jit_solution(8078569418516562766)
XLA Ops:
  0.0 1.3 %broadcast_in_dim.6.gain_ref = f32[1,3584]{1,0:T(1,128)} reshape(f32[3584]{0:T(1024)} %param.10) | data formatting | bytes 28672 | tf_op jit(solution)/shard_map/broadcast_in_dim | solution.py:344
  1.3 1.4 %copy.10.routes_ref = s32[64,8]{1,0:T(8,128)} copy(s32[64,8]{0,1:T(8,128)} %param.12) | data formatting | bytes 4096 | tf_op args[4]
  2.7 1.9 %copy.9.router_ref = bf16[1792,64]{1,0:T(8,128)(2,1)} copy(bf16[1792,64]{0,1:T(8,128)(2,1)} %param.11) | data formatting | bytes 458752 | tf_op args[3]
  4.6 69.0 %shard_map.82 = bf16[64,1792]{1,0:T(8,128)(2,1)} custom-call(bf16[64,3584]{1,0:T(8,128)(2,1)} %res_ref.1, bf16[1,64,3584]{2,1,0:T(8,128)(2,1)} %dense_ref.1, f32[1,3584]{1,0:T(1,128)} %broadcast_in_dim.6.gain_ref, bf16[1792,64]{1,0:T(8,128)(2,1)} %copy.9.router_ref, s32[64,8]{1,0:T(8,128)} %copy.10.routes_ref, s32[1,64]{1,0:T(1,128)} %bitcast.1, ...), custom_call_target="tpu_custom_call" | custom-call | tf_op jit(solution)/shard_map/pallas_call | solution.py:308
  73.6 1.6 %copy.12 = bf16[64,1792]{1,0:T(8,128)(2,1)} copy(bf16[64,1792]{1,0:T(8,128)(2,1)} %shard_map.82) | data formatting | bytes 458752

commit v4 on v3

--- a/solution.py
+++ b/solution.py
@@ -33,11 +33,11 @@
 
 def expert_kernel(
     slots, res_ref, dense_ref, gain_ref, router_ref, routes_ref, place_ref, up_ref, down_ref, out_ref,
-    theirs, state, stat_own, stat_peer, d_send, d_recv, gather, xy, pre_own, pre_peer, sel, sel_t, gate_col,
+    gain_row, theirs, state, stat_own, stat_peer, d_send, d_recv, gather, xy, pre_own, pre_peer, sel, sel_t, gate_col,
     send_buf, recv_buf, up_buf, down_buf, up_sem, down_sem, g_send, g_recv, p_send, p_recv, r_send, r_recv,
 ):
     tok, full_width = res_ref.shape
-    experts = router_ref.shape[1]
+    experts = router_ref.shape[0]
     width_ext = gather.shape[2]
     part_w = down_buf.shape[2]
     width = part_w * PARTS
@@ -86,6 +86,7 @@
         down_copy(j).start()
     pl.semaphore_wait(barrier, 3)
 
+    gain_row[...] = gain_ref[...].reshape(1, full_width)
     mine = pl.ds(pl.multiple_of(tp * width, width), width)
     other = pl.ds(pl.multiple_of((1 - tp) * width, width), width)
     dense_copy = pltpu.make_async_remote_copy(
@@ -98,9 +99,10 @@
     dense_copy.wait()
     total = partial + (own_dense + theirs[...].astype(F32))
     state[...] = total
-    scaled = total * gain_ref[:, mine]
-    stat_own[:, :experts] = jnp.dot(
-        scaled, router_ref[...].astype(F32), precision=lax.Precision.HIGHEST, preferred_element_type=F32
+    scaled = total * gain_row[:, mine]
+    stat_own[:, :experts] = lax.dot_general(
+        scaled, router_ref[...].astype(F32), (((1,), (1,)), ((), ())),
+        precision=lax.Precision.HIGHEST, preferred_element_type=F32,
     )
     square = jnp.sum(total * total, axis=1, keepdims=True)
     stat_own[:, experts:] = jnp.broadcast_to(square, (tok, stat_own.shape[1] - experts))
@@ -109,17 +111,19 @@
         device_id={"tp": 1 - tp}, device_id_type=MESH,
     )
     stat_copy.start()
-    expert_id = lax.broadcasted_iota(jnp.int32, (tok, experts), 1)
-    routed = routes_ref[:, 0:1] == expert_id
-    for r in range(1, routes_ref.shape[1]):
-        routed = routed | (routes_ref[:, r : r + 1] == expert_id)
+    expert_id = lax.broadcasted_iota(jnp.int32, (experts, tok), 0)
+    routed_t = routes_ref[0:1, :] == expert_id
+    for r in range(1, routes_ref.shape[0]):
+        routed_t = routed_t | (routes_ref[r : r + 1, :] == expert_id)
+    same = lax.broadcasted_iota(jnp.int32, (tok, tok), 0) == lax.broadcasted_iota(jnp.int32, (tok, tok), 1)
+    routed = nt_dot(same.astype(F32).astype(BF16), routed_t.astype(F32).astype(BF16)) > 0.0
     table = place_ref[...] == lax.broadcasted_iota(jnp.int32, (experts, experts), 0)
     table = table.astype(F32).astype(BF16)
     stat_copy.wait()
     logits = stat_own[:, :experts] + stat_peer[:, :experts]
     mean_sq = (stat_own[:, experts : experts + 1] + stat_peer[:, experts : experts + 1]) / full_width
     scale = lax.rsqrt(mean_sq + 1e-06)
-    gather[pos, :, :width] = (state[...] * gain_ref[:, mine] * scale).astype(BF16)
+    gather[pos, :, :width] = (state[...] * gain_row[:, mine] * scale).astype(BF16)
     chosen = jnp.where(routed, jax.nn.sigmoid(logits * scale), 0.0)
     gate = 2.827 * chosen / jnp.sum(chosen, axis=1, keepdims=True)
     high = gate.astype(BF16)
@@ -311,6 +315,7 @@
         in_specs=[vmem] * 6 + [hbm, hbm],
         out_specs=vmem,
         scratch_shapes=[
+            pltpu.VMEM((1, residual_in.shape[1]), F32),
             pltpu.VMEM((tok, width), BF16),
             pltpu.VMEM((tok, width), F32),
             pltpu.VMEM((tok, 2 * experts), F32),
@@ -341,7 +346,7 @@
             collective_id=0, has_side_effects=True, vmem_limit_bytes=62 * 1024 * 1024
         ),
     )(
-        residual_in, dense_terms, norm_gain[None], router_weight, routes, placement[None], up_weight, down_weight
+        residual_in, dense_terms, norm_gain, router_weight.T, routes.T, placement[None], up_weight, down_weight
     )
 
 

time: 75.6 us -> 71.2 us (0.942)
  local copies, waits for them, and re-layouts: 6.27 us -> 1.64 us
    unnamed x3 -> x1, local copies, waits for them, and re-layouts: 4.94 us -> 1.64 us
    broadcast_in_dim x1 -> x0, local copies, waits for them, and re-layouts: 1.32 us -> none  [block_on_ring(): norm_gain[None]]
where the time goes in v4:
time: 71.2 us; the launch traced here: 71 us
  Pallas kernels  69.4 us (97%)
  local copies, waits for them, and re-layouts  1.64 us (2%)
    pallas_call x1, Pallas kernels, block_on_ring(): pl.pallas_call(functools.partial(expert_kernel, slots), out_shape=jax.Sha...  69.4 us
    unnamed x1, local copies, waits for them, and re-layouts  1.64 us

profile of v4, /device:TPU:0, one launch (start us, length us, event | category | flops | bytes accessed | tf_op | source)
XLA Modules:
  0.0 71.0 jit_solution(2085035015015850117)
XLA Ops:
  0.0 69.4 %shard_map.82 = bf16[64,1792]{1,0:T(8,128)(2,1)} custom-call(bf16[64,3584]{1,0:T(8,128)(2,1)} %res_ref.1, bf16[1,64,3584]{2,1,0:T(8,128)(2,1)} %dense_ref.1, f32[3584]{0:T(1024)} %gain_ref.1, bf16[64,1792]{1,0:T(8,128)(2,1)} %bitcast.3, s32[8,64]{1,0:T(8,128)} %bitcast.4, s32[1,64]{1,0:T(1,128)} %bitcast.5, bf16[1792,8192]{1,0:T(8,128)(2,1)} %up_ref.1, ...), custom_call_target="tpu_custom_call" | custom-call | tf_op jit(solution)/shard_map/pallas_call | solution.py:312
  69.4 1.6 %copy.10 = bf16[64,1792]{1,0:T(8,128)(2,1)} copy(bf16[64,1792]{1,0:T(8,128)(2,1)} %shard_map.82) | data formatting | bytes 458752

commit v5 on v4

--- a/solution.py
+++ b/solution.py
@@ -13,6 +13,7 @@
 UP_BUFS = 6
 DOWN_BUFS = 12
 PARTS = 2
+ROW_PARTS = 4
 MESH = pl.DeviceIdType.MESH
 F32 = jnp.float32
 BF16 = jnp.bfloat16
@@ -46,6 +47,7 @@
     total_rows = slots * cap
     tokens = tok * RING
     half = tok // 2
+    piece = tok // ROW_PARTS
 
     ep = lax.axis_index("ep")
     tp = lax.axis_index("tp")
@@ -133,7 +135,7 @@
 
     def gather_copy(way, k, c):
         block = lax.rem(pos - step_of[way] * k + RING, RING)
-        ref = gather.at[block, pl.ds(c * half, half), :]
+        ref = gather.at[block, pl.ds(c * piece, piece), :]
         return pltpu.make_async_remote_copy(
             src_ref=ref, dst_ref=ref, send_sem=g_send.at[way, k, c], recv_sem=g_recv.at[way, k, c],
             device_id={"ep": sides[way]}, device_id_type=MESH,
@@ -142,17 +144,18 @@
     steps = RING // 2
     copies = {}
     for k in range(steps):
-        for c in range(PARTS):
+        for c in range(ROW_PARTS):
             for way in range(2):
-                part = way if c == 0 else 1 - way
+                part = (c + way * (ROW_PARTS // 2)) % ROW_PARTS
                 if k:
                     copies[way, k - 1, part].wait_recv()
-                if k == steps - 1 and part != way:
+                if k == steps - 1 and c >= ROW_PARTS // 2:
                     continue
                 copies[way, k, part] = gather_copy(way, k, part)
                 copies[way, k, part].start()
     for way in range(2):
-        copies[way, steps - 1, way].wait_recv()
+        for c in range(ROW_PARTS // 2):
+            copies[way, steps - 1, c + way * (ROW_PARTS // 2)].wait_recv()
     for copy in copies.values():
         copy.wait_send()
 
@@ -335,8 +338,8 @@
             pltpu.VMEM((DOWN_BUFS, FF_E, width // PARTS), BF16),
             dma((UP_BUFS,)),
             dma((DOWN_BUFS,)),
-            dma((2, steps, PARTS)),
-            dma((2, steps, PARTS)),
+            dma((2, steps, ROW_PARTS)),
+            dma((2, steps, ROW_PARTS)),
             dma((slots,)),
             dma((slots,)),
             dma((2, steps, PARTS)),

time: 71.2 us -> 71.5 us (level)
  no operation moved by 1% of the time
where the time goes in v5:
time: 71.5 us; the launch traced here: 71.3 us
  Pallas kernels  69.7 us (97%)
  local copies, waits for them, and re-layouts  1.64 us (2%)
    pallas_call x1, Pallas kernels, block_on_ring(): pl.pallas_call(functools.partial(expert_kernel, slots), out_shape=jax.Sha...  69.7 us
    unnamed x1, local copies, waits for them, and re-layouts  1.64 us

profile of v5, /device:TPU:0, one launch (start us, length us, event | category | flops | bytes accessed | tf_op | source)
XLA Modules:
  0.0 71.3 jit_solution(16827617106994148227)
XLA Ops:
  0.0 69.7 %shard_map.82 = bf16[64,1792]{1,0:T(8,128)(2,1)} custom-call(bf16[64,3584]{1,0:T(8,128)(2,1)} %res_ref.1, bf16[1,64,3584]{2,1,0:T(8,128)(2,1)} %dense_ref.1, f32[3584]{0:T(1024)} %gain_ref.1, bf16[64,1792]{1,0:T(8,128)(2,1)} %bitcast.3, s32[8,64]{1,0:T(8,128)} %bitcast.4, s32[1,64]{1,0:T(1,128)} %bitcast.5, bf16[1792,8192]{1,0:T(8,128)(2,1)} %up_ref.1, ...), custom_call_target="tpu_custom_call" | custom-call | tf_op jit(solution)/shard_map/pallas_call | solution.py:315
  69.7 1.6 %copy.10 = bf16[64,1792]{1,0:T(8,128)(2,1)} copy(bf16[64,1792]{1,0:T(8,128)(2,1)} %shard_map.82) | data formatting | bytes 458752
